TPU v7x, 256 devices: a whole 4x4x8 slice. The times are simulated.
256 devices in a mesh: prow: 8 (over x, core), pcol: 32 (over y, z).
Axes of the slice: x: 4, y: 4, z: 8, core: 2. Of those that a mesh axis runs over, the one named last changes fastest.
Arguments:
- factor_blocks: float32 [6, 4, 8, 32, 256, 256], P(None, None, 'prow', 'pcol'), may hold values from -0.03125 to 0.03125
- block_pattern: int32 [6, 4, 8, 32], P(None, None, 'prow', 'pcol'), may hold values 0 or 1
- right_side: float32 [4, 32, 512, 256], P(None, 'pcol'), may hold values from -6 to 6
- diag_inverse: float32 [4, 32, 256, 256], P(None, 'pcol'), may hold values from -1 to 1.5, as said below
Outputs:
- forward_solution: float32 [4, 32, 512, 256], P(None, 'pcol')
- solution: float32 [4, 32, 512, 256], P(None, 'pcol', 'prow')
Inputs may be any that keep to these rules, and one draw needn't show every extreme that they name: Each block of diag_inverse is lower triangular with diagonal entries from 0.5 to 1.5.
All inputs are finite; a program needn't handle non-finite values. No bound on the sum of `block_pattern` on one device may be relied on, other than what follows from the above.
Results may differ from a plain program's by a relative error of at most 0.0001.
Values sent between devices are 32-bit elements; how exact they have to be, the bound alone decides.
No kernel may reach another device: no remote copies, remote signals or barrier semaphores. Data moves between devices by JAX's collectives and lax.ppermute only.
A program may use at most 64 MiB of HBM per device.

v0:
```python
import jax
import jax.numpy as jnp
from jax import lax
from jax.sharding import PartitionSpec as P

B = 256
NRHS = 512
LV = 4
highest = lax.Precision.HIGHEST


def from_root(value, axis, source):
    kept = jnp.where(lax.axis_index(axis) == source, value, 0).astype(value.dtype)
    return lax.psum(kept, axis)


def pair_number(later_level, earlier):
    return later_level * (later_level - 1) // 2 + earlier


def deliver_update(partial_sum, own_column, row_count):
    summed = lax.psum(partial_sum, "pcol")
    picked = lax.dynamic_index_in_dim(summed, own_column // row_count, 0, keepdims=False)
    return from_root(picked, "prow", own_column % row_count)


def collect_column(partial_sum, own_row, side_share):
    summed = lax.psum(partial_sum, "prow")
    return lax.dynamic_slice_in_dim(summed, own_row * side_share, side_share, 0)


def local(factor_blocks, block_pattern, right_side, diag_inverse):
    row_count = lax.axis_size("prow")
    own_row = lax.axis_index("prow")
    own_column = lax.axis_index("pcol")
    per_row = factor_blocks.shape[1]
    side_share = NRHS // row_count
    pattern_float = block_pattern[:, :, 0, 0].astype(jnp.float32)
    local_blocks = factor_blocks[:, :, 0, 0]
    own_right = right_side[:, 0]
    own_inverse = diag_inverse[:, 0]
    forward = []
    for current in range(LV):
        if current == 0:
            arrived = jnp.zeros((NRHS, B), jnp.float32)
        else:
            partial_sum = jnp.zeros((per_row, NRHS, B), jnp.float32)
            for earlier in range(current):
                number = pair_number(current, earlier)
                partial_sum = partial_sum + jnp.einsum(
                    "nj,aij,a->ani",
                    forward[earlier],
                    local_blocks[number],
                    pattern_float[number],
                    precision=highest,
                )
            arrived = deliver_update(partial_sum, own_column, row_count)
        solved = lax.dot_general(
            own_right[current] - arrived,
            own_inverse[current],
            (((1,), (1,)), ((), ())),
            precision=highest,
            preferred_element_type=jnp.float32,
        )
        forward.append(solved)
    solution = [None] * LV
    arrived_rows = [None] * LV
    for current in range(LV - 1, -1, -1):
        own_slice = lax.dynamic_slice_in_dim(forward[current], own_row * side_share, side_share, 0)
        if current == LV - 1:
            share_update = jnp.zeros((side_share, B), jnp.float32)
        else:
            partial_sum = jnp.zeros((NRHS, B), jnp.float32)
            for later_level in range(current + 1, LV):
                number = pair_number(later_level, current)
                partial_sum = partial_sum + jnp.einsum(
                    "ani,aij,a->nj",
                    arrived_rows[later_level],
                    local_blocks[number],
                    pattern_float[number],
                    precision=highest,
                )
            share_update = collect_column(partial_sum, own_row, side_share)
        solved = jnp.dot(
            own_slice - share_update,
            own_inverse[current],
            precision=highest,
            preferred_element_type=jnp.float32,
        )
        solution[current] = solved
        if current > 0:
            gathered = lax.all_gather(solved[None], "pcol", axis=0, tiled=True)
            grouped = gathered.reshape(per_row, row_count, side_share, B)
            delivered = lax.all_to_all(grouped, "prow", split_axis=1, concat_axis=2, tiled=True)
            arrived_rows[current] = delivered[:, 0]
    return (jnp.stack(forward)[:, None], jnp.stack(solution)[:, None])


def solution(mesh):
    in_specs = (
        P(None, None, "prow", "pcol", None, None),
        P(None, None, "prow", "pcol"),
        P(None, "pcol", None, None),
        P(None, "pcol", None, None),
    )
    out_specs = (P(None, "pcol", None, None), P(None, "pcol", "prow", None))
    return jax.shard_map(local, mesh=mesh, in_specs=in_specs, out_specs=out_specs, check_vma=False)
```

profile of v0, /device:TPU:8, one launch (start us, length us, event | category | flops | bytes accessed | tf_op | source)
XLA Modules:
  0.0 1243.7 jit_solution(7310851583592979462)
XLA Ops:
  9.8 4.5 convolution_bitcast_fusion
  16.6 153.7 %all-reduce.10.cloned.1.call-done = f32[4,512,256]{1,2,0:T(8,128)} async-done(((f32[4,512,256]{1,2,0:T(8,128)}), f32[4,512,256]{1,2,0:T(8,128)}) %all-reduce.10.cloned.1.call-update) | async-done | bytes 2097168 | tf_op jit(solution)/shard_map/psum | solution.py:22
  175.3 62.1 %all-reduce.12.cloned.1.call-done = f32[512,256]{0,1:T(8,128)} async-done(((f32[512,256]{0,1:T(8,128)}), f32[512,256]{0,1:T(8,128)}) %all-reduce.12.cloned.1.call-update) | async-done | bytes 524304 | tf_op jit(solution)/shard_map/psum | solution.py:14
  239.7 4.4 add_bitcast_fusion.1
  249.2 147.1 %all-reduce.14.cloned.1.call-done = f32[4,512,256]{1,2,0:T(8,128)} async-done(((f32[4,512,256]{1,2,0:T(8,128)}), f32[4,512,256]{1,2,0:T(8,128)}) %all-reduce.14.cloned.1.call-update) | async-done | bytes 2097168 | tf_op jit(solution)/shard_map/psum | solution.py:22
  398.5 4.4 fusion.5
  402.9 59.9 %all-reduce.16.cloned.1.call-done = f32[512,256]{0,1:T(8,128)} async-done(((f32[512,256]{0,1:T(8,128)}), f32[512,256]{0,1:T(8,128)}) %all-reduce.16.cloned.1.call-update) | async-done | bytes 524304 | tf_op jit(solution)/shard_map/psum | solution.py:14
  465.8 5.2 add_bitcast_fusion
  471.1 152.2 %all-reduce.18.cloned.1.call-done = f32[4,512,256]{1,2,0:T(8,128)} async-done(((f32[4,512,256]{1,2,0:T(8,128)}), f32[4,512,256]{1,2,0:T(8,128)}) %all-reduce.18.cloned.1.call-update) | async-done | bytes 2097168 | tf_op jit(solution)/shard_map/psum | solution.py:22
  625.5 64.8 %all-reduce.20.cloned.1.call-done = f32[512,256]{0,1:T(8,128)} async-done(((f32[512,256]{0,1:T(8,128)}), f32[512,256]{0,1:T(8,128)}) %all-reduce.20.cloned.1.call-update) | async-done | bytes 524304 | tf_op jit(solution)/shard_map/psum | solution.py:14
  694.1 76.1 %all-gather.7.cloned.1.call-done = f32[2048,256]{1,0:T(8,128)} async-done(((f32[64,256]{1,0:T(8,128)}), f32[2048,256]{1,0:T(8,128)}) %all-gather.7.cloned.1.call-update) | async-done | bytes 2097168 | tf_op jit(solution)/shard_map/all_gather | solution.py:92
  771.9 31.6 %all_to_all.12 = f32[4,8,64,256]{3,2,0,1:T(8,128)S(1)} all-to-all(f32[4,8,64,256]{3,2,0,1:T(8,128)S(1)} %copy.19), channel_id=1, replica_groups=mesh['prow'=8,'pcol'=32] {'prow'}, dimensions={1} | all-to-all | bytes 4194304 | tf_op jit(solution)/shard_map/all_to_all | solution.py:94
  807.7 62.3 %all-reduce.22.cloned.1.call-done = f32[512,256]{1,0:T(8,128)} async-done(((f32[512,256]{1,0:T(8,128)}), f32[512,256]{1,0:T(8,128)}) %all-reduce.22.cloned.1.call-update) | async-done | bytes 524304 | tf_op jit(solution)/shard_map/psum | solution.py:28
  871.9 77.0 %all-gather.9.cloned.1.call-done = f32[2048,256]{1,0:T(8,128)} async-done(((f32[64,256]{1,0:T(8,128)}), f32[2048,256]{1,0:T(8,128)}) %all-gather.9.cloned.1.call-update) | async-done | bytes 2097168 | tf_op jit(solution)/shard_map/all_gather | solution.py:92
  952.1 4.4 all-to-all-start.1
  960.7 23.0 %all-to-all-done.1 = f32[4,8,64,256]{3,2,0,1:T(8,128)} async-done(((f32[4,8,64,256]{3,2,0,1:T(8,128)}), f32[4,8,64,256]{3,2,0,1:T(8,128)}, u32[]{:S(2)}, u32[]{:S(2)}) %all-to-all-start.1) | async-done | bytes 2097184 | tf_op jit(solution)/shard_map/all_to_all | solution.py:94
  986.8 4.0 fusion
  990.8 62.5 %all-reduce.24.cloned.1.call-done = f32[512,256]{1,0:T(8,128)} async-done(((f32[512,256]{1,0:T(8,128)}), f32[512,256]{1,0:T(8,128)}) %all-reduce.24.cloned.1.call-update) | async-done | bytes 524304 | tf_op jit(solution)/shard_map/psum | solution.py:28
  1055.1 76.7 %all-gather.11.cloned.1.call-done = f32[2048,256]{1,0:T(8,128)} async-done(((f32[64,256]{1,0:T(8,128)}), f32[2048,256]{1,0:T(8,128)}) %all-gather.11.cloned.1.call-update) | async-done | bytes 2097168 | tf_op jit(solution)/shard_map/all_gather | solution.py:92
  1135.0 4.3 all-to-all-start.2
  1139.4 4.1 convolution_bitcast_fusion.1
  1146.7 19.9 %all-to-all-done.2 = f32[4,8,64,256]{3,2,0,1:T(8,128)} async-done(((f32[4,8,64,256]{3,2,0,1:T(8,128)}), f32[4,8,64,256]{3,2,0,1:T(8,128)}, u32[]{:S(2)}, u32[]{:S(2)}) %all-to-all-start.2) | async-done | bytes 2097184 | tf_op jit(solution)/shard_map/all_to_all | solution.py:94
  1168.4 4.0 fusion.2
  1174.0 60.9 %all-reduce.26.cloned.1.call-done = f32[512,256]{1,0:T(8,128)} async-done(((f32[512,256]{1,0:T(8,128)}), f32[512,256]{1,0:T(8,128)}) %all-reduce.26.cloned.1.call-update) | async-done | bytes 524304 | tf_op jit(solution)/shard_map/psum | solution.py:28
  (84 shorter events, 60.0 us)
Async XLA Ops:
  7.2 163.1 %all-reduce.10.cloned.1.call-start = ((), (), s32[]{:S(2)}) async-start(), calls=%async_computation.3 | async-start | bytes 4194304 | tf_op jit(solution)/shard_map/psum | solution.py:22
  9.8 4.7 copy-start.7
  14.4 223.0 %all-reduce.12.cloned.1.call-start = ((), (), s32[]{:S(2)}) async-start(), calls=%async_computation.4 | async-start | bytes 1048576 | tf_op jit(solution)/shard_map/psum | solution.py:14
  172.2 224.2 %all-reduce.14.cloned.1.call-start = ((), (), s32[]{:S(2)}) async-start(), calls=%async_computation.5 | async-start | bytes 4194304 | tf_op jit(solution)/shard_map/psum | solution.py:22
  244.1 218.6 %all-reduce.16.cloned.1.call-start = ((), (), s32[]{:S(2)}) async-start(), calls=%async_computation.6 | async-start | bytes 1048576 | tf_op jit(solution)/shard_map/psum | solution.py:14
  398.2 225.1 %all-reduce.18.cloned.1.call-start = ((), (), s32[]{:S(2)}) async-start(), calls=%async_computation.7 | async-start | bytes 4194304 | tf_op jit(solution)/shard_map/psum | solution.py:22
  471.0 154.2 %copy-start.10 = (f32[1,1,512,256]{3,2,1,0:T(8,128)S(1)}, f32[1,1,512,256]{3,2,1,0:T(8,128)}, u32[]{:S(2)}) copy-start(f32[1,1,512,256]{3,2,1,0:T(8,128)} %get-tuple-element.14) | copy-start | bytes 1572868
  471.0 219.3 %copy-start.4 = (f32[4,1,256,256]{3,2,1,0:T(8,128)S(1)}, f32[4,1,256,256]{3,2,1,0:T(8,128)}, u32[]{:S(2)}) copy-start(f32[4,1,256,256]{3,2,1,0:T(8,128)} %param.7) | copy-start | bytes 3145732
  471.0 219.3 %all-reduce.20.cloned.1.call-start = ((), (), s32[]{:S(2)}) async-start(), calls=%async_computation.8 | async-start | bytes 1048576 | tf_op jit(solution)/shard_map/psum | solution.py:14
  625.2 145.0 %all-gather.7.cloned.1.call-start = ((), (), s32[]{:S(2)}) async-start(), calls=%async_computation.12 | async-start | bytes 2162688 | tf_op jit(solution)/shard_map/all_gather | solution.py:92
  694.0 175.9 %all-reduce.22.cloned.1.call-start = ((), (), s32[]{:S(2)}) async-start(), calls=%async_computation.9 | async-start | bytes 1048576 | tf_op jit(solution)/shard_map/psum | solution.py:28
  807.6 141.4 %all-gather.9.cloned.1.call-start = ((), (), s32[]{:S(2)}) async-start(), calls=%async_computation.13 | async-start | bytes 2162688 | tf_op jit(solution)/shard_map/all_gather | solution.py:92
  952.1 31.6 %all-to-all-start.1 = ((f32[4,8,64,256]{3,2,0,1:T(8,128)}), f32[4,8,64,256]{3,2,0,1:T(8,128)}, u32[]{:S(2)}, u32[]{:S(2)}) async-start(f32[4,8,64,256]{3,2,0,1:T(8,128)} %copy.21), calls=%async_computation.1 | async-start | bytes 4194304 | tf_op jit(solution)/shard_map/all_to_all | solution.py:94
  956.4 96.8 %all-reduce.24.cloned.1.call-start = ((), (), s32[]{:S(2)}) async-start(), calls=%async_computation.10 | async-start | bytes 1048576 | tf_op jit(solution)/shard_map/psum | solution.py:28
  990.7 141.1 %all-gather.11.cloned.1.call-start = ((), (), s32[]{:S(2)}) async-start(), calls=%async_computation.14 | async-start | bytes 2162688 | tf_op jit(solution)/shard_map/all_gather | solution.py:92
  1135.0 31.6 %all-to-all-start.2 = ((f32[4,8,64,256]{3,2,0,1:T(8,128)}), f32[4,8,64,256]{3,2,0,1:T(8,128)}, u32[]{:S(2)}, u32[]{:S(2)}) async-start(f32[4,8,64,256]{3,2,0,1:T(8,128)} %copy.23), calls=%async_computation.2 | async-start | bytes 4194304 | tf_op jit(solution)/shard_map/all_to_all | solution.py:94
  1139.4 95.5 %all-reduce.26.cloned.1.call-start = ((), (), s32[]{:S(2)}) async-start(), calls=%async_computation.11 | async-start | bytes 1048576 | tf_op jit(solution)/shard_map/psum | solution.py:28
  1139.4 4.2 copy-start.1
  1146.7 21.6 %copy-start.8 = (f32[512,256]{1,0:T(8,128)S(1)}, f32[512,256]{1,0:T(8,128)}, u32[]{:S(2)}) copy-start(f32[512,256]{1,0:T(8,128)} %convolution_bitcast_fusion.1) | copy-start | bytes 1572868
  1168.3 4.1 copy-start.3
  1168.3 4.1 copy-start.6
  1172.4 63.7 %copy-start.12 = (f32[64,256]{1,0:T(8,128)S(1)}, f32[64,256]{1,0:T(8,128)}, u32[]{:S(2)}) copy-start(f32[64,256]{1,0:T(8,128)} %fusion.30) | copy-start | bytes 196612
  1172.5 63.7 %copy-start.13 = (f32[64,256]{1,0:T(8,128)S(1)}, f32[64,256]{1,0:T(8,128)}, u32[]{:S(2)}) copy-start(f32[64,256]{1,0:T(8,128)} %fusion.33) | copy-start | bytes 196612
  1172.5 63.7 %copy-start.14 = (f32[64,256]{1,0:T(8,128)S(1)}, f32[64,256]{1,0:T(8,128)}, u32[]{:S(2)}) copy-start(f32[64,256]{1,0:T(8,128)} %fusion.36) | copy-start | bytes 196612
  (5 other events, 7.1 us)
Sparse Core Ops, SparseCore 0:
  14.5 155.6 all-reduce.9
  173.3 64.0 all-reduce.11
  244.2 152.0 all-reduce.13
  398.6 64.0 all-reduce.15
  471.2 152.0 all-reduce.17
  626.2 64.0 all-reduce.19
  694.2 75.9 all-gather.6
  807.7 62.2 all-reduce.21
  872.9 75.9 all-gather.8
  990.9 62.3 all-reduce.23
  1055.9 75.9 all-gather.10
  1172.5 62.2 all-reduce.25
where the time goes:
time: 1240 us
  waiting for transfers between devices  1100 us (89%)
  matrix products  62 us (5%)
  blocking collectives  31.6 us (3%)
  local copies, waits for them, and re-layouts  19 us (2%)
  between operations  14.5 us (1%)
    psum x3, waiting for transfers between devices, deliver_update(): summed = lax.psum(partial_sum, 'pcol')  453 us
    all_gather x3, waiting for transfers between devices, local(): gathered = lax.all_gather(solved[None], 'pcol', axis=0, tiled=True)  230 us
    psum x3, waiting for transfers between devices, from_root(): return lax.psum(kept, axis)  187 us
    psum x3, waiting for transfers between devices, collect_column(): summed = lax.psum(partial_sum, 'prow')  186 us
    all_to_all x2, waiting for transfers between devices, local(): lax.all_to_all(grouped, 'prow', split_axis=1, concat_axis=2, tiled=True)  42.8 us
    all_to_all x1, blocking collectives, local(): lax.all_to_all(grouped, 'prow', split_axis=1, concat_axis=2, tiled=True)  31.6 us
  transfers between devices with their start and end apart: 14, of which 14 were waited for; matrix products, arithmetic and copies ran while one was open for 2% of the time, Pallas kernels for 0%

commit v1 on v0

--- a/solution.py
+++ b/solution.py
@@ -11,7 +11,7 @@
 
 def from_root(value, axis, source):
     kept = jnp.where(lax.axis_index(axis) == source, value, 0).astype(value.dtype)
-    return lax.psum(kept, axis)
+    return jnp.sum(lax.all_gather(kept, axis), axis=0)
 
 
 def pair_number(later_level, earlier):

time: 1240 us -> 1170 us (0.944)
  waiting for transfers between devices: 1100 us -> 1010 us
    psum x3 -> x0, waiting for transfers between devices: 187 us -> none  [from_root(): return lax.psum(kept, axis)]
    all_gather x0 -> x3, waiting for transfers between devices: none -> 85.6 us  [from_root(): return jnp.sum(lax.all_gather(kept, axis), axis=0)]
where the time goes in v1:
time: 1170 us; the launch traced here: 1160 us
  waiting for transfers between devices  1010 us (86%)
  matrix products  61.9 us (5%)
  blocking collectives  31.6 us (3%)
  local copies, waits for them, and re-layouts  25.2 us (2%)
  other arithmetic  14.5 us (1%)
  between operations  14.5 us (1%)
    psum x3, waiting for transfers between devices, deliver_update(): summed = lax.psum(partial_sum, 'pcol')  462 us
    all_gather x3, waiting for transfers between devices, local(): gathered = lax.all_gather(solved[None], 'pcol', axis=0, tiled=True)  231 us
    psum x3, waiting for transfers between devices, collect_column(): summed = lax.psum(partial_sum, 'prow')  186 us
    all_gather x3, waiting for transfers between devices, from_root(): return jnp.sum(lax.all_gather(kept, axis), axis=0)  85.6 us
    all_to_all x2, waiting for transfers between devices, local(): lax.all_to_all(grouped, 'prow', split_axis=1, concat_axis=2, tiled=True)  43.1 us
    all_to_all x1, blocking collectives, local(): lax.all_to_all(grouped, 'prow', split_axis=1, concat_axis=2, tiled=True)  31.6 us
    dot_general x6, matrix products, local(): jnp.einsum('nj,aij,a->ani', forward[earlier], local_blocks[number], patte...  24.5 us
  transfers between devices with their start and end apart: 14, of which 14 were waited for; matrix products, arithmetic and copies ran while one was open for 2% of the time, Pallas kernels for 0%

profile of v1, /device:TPU:8, one launch (start us, length us, event | category | flops | bytes accessed | tf_op | source)
XLA Modules:
  0.0 1163.8 jit_solution(10399179740021085006)
XLA Ops:
  9.8 4.4 convolution_bitcast_fusion
  14.3 155.8 %all-reduce.7.cloned.1.call-done = f32[4,512,256]{1,2,0:T(8,128)} async-done(((f32[4,512,256]{1,2,0:T(8,128)}), f32[4,512,256]{1,2,0:T(8,128)}) %all-reduce.7.cloned.1.call-update) | async-done | bytes 2097168 | tf_op jit(solution)/shard_map/psum | solution.py:22
  177.5 28.0 %all-gather.10.cloned.1.call-done = f32[8,512,256]{2,1,0:T(8,128)} async-done(((f32[1,512,256]{2,1,0:T(8,128)}), f32[8,512,256]{2,1,0:T(8,128)}) %all-gather.10.cloned.1.call-update) | async-done | bytes 4194320 | tf_op jit(solution)/shard_map/all_gather | solution.py:14
  211.2 4.4 add_bitcast_fusion.1
  215.7 152.9 %all-reduce.9.cloned.1.call-done = f32[4,512,256]{1,2,0:T(8,128)} async-done(((f32[4,512,256]{1,2,0:T(8,128)}), f32[4,512,256]{1,2,0:T(8,128)}) %all-reduce.9.cloned.1.call-update) | async-done | bytes 2097168 | tf_op jit(solution)/shard_map/psum | solution.py:22
  375.1 4.4 fusion.5
  379.5 24.5 %all-gather.12.cloned.1.call-done = f32[8,512,256]{2,1,0:T(8,128)} async-done(((f32[1,512,256]{2,1,0:T(8,128)}), f32[8,512,256]{2,1,0:T(8,128)}) %all-gather.12.cloned.1.call-update) | async-done | bytes 4194320 | tf_op jit(solution)/shard_map/all_gather | solution.py:14
  412.5 5.2 add_bitcast_fusion
  417.7 152.9 %all-reduce.11.cloned.1.call-done = f32[4,512,256]{1,2,0:T(8,128)} async-done(((f32[4,512,256]{1,2,0:T(8,128)}), f32[4,512,256]{1,2,0:T(8,128)}) %all-reduce.11.cloned.1.call-update) | async-done | bytes 2097168 | tf_op jit(solution)/shard_map/psum | solution.py:22
  573.1 33.1 %all-gather.14.cloned.1.call-done = f32[8,512,256]{2,1,0:T(8,128)} async-done(((f32[1,512,256]{2,1,0:T(8,128)}), f32[8,512,256]{2,1,0:T(8,128)}) %all-gather.14.cloned.1.call-update) | async-done | bytes 4194320 | tf_op jit(solution)/shard_map/all_gather | solution.py:14
  613.5 76.8 %all-gather.16.cloned.1.call-done = f32[2048,256]{1,0:T(8,128)} async-done(((f32[64,256]{1,0:T(8,128)}), f32[2048,256]{1,0:T(8,128)}) %all-gather.16.cloned.1.call-update) | async-done | bytes 2097168 | tf_op jit(solution)/shard_map/all_gather | solution.py:92
  692.1 31.6 %all_to_all.12 = f32[4,8,64,256]{3,2,0,1:T(8,128)S(1)} all-to-all(f32[4,8,64,256]{3,2,0,1:T(8,128)S(1)} %copy.19), channel_id=1, replica_groups=mesh['prow'=8,'pcol'=32] {'prow'}, dimensions={1} | all-to-all | bytes 4194304 | tf_op jit(solution)/shard_map/all_to_all | solution.py:94
  727.8 62.4 %all-reduce.13.cloned.1.call-done = f32[512,256]{1,0:T(8,128)} async-done(((f32[512,256]{1,0:T(8,128)}), f32[512,256]{1,0:T(8,128)}) %all-reduce.13.cloned.1.call-update) | async-done | bytes 524304 | tf_op jit(solution)/shard_map/psum | solution.py:28
  792.1 76.7 %all-gather.18.cloned.1.call-done = f32[2048,256]{1,0:T(8,128)} async-done(((f32[64,256]{1,0:T(8,128)}), f32[2048,256]{1,0:T(8,128)}) %all-gather.18.cloned.1.call-update) | async-done | bytes 2097168 | tf_op jit(solution)/shard_map/all_gather | solution.py:92
  871.9 4.4 all-to-all-start.1
  880.3 23.2 %all-to-all-done.1 = f32[4,8,64,256]{3,2,0,1:T(8,128)} async-done(((f32[4,8,64,256]{3,2,0,1:T(8,128)}), f32[4,8,64,256]{3,2,0,1:T(8,128)}, u32[]{:S(2)}, u32[]{:S(2)}) %all-to-all-start.1) | async-done | bytes 2097184 | tf_op jit(solution)/shard_map/all_to_all | solution.py:94
  906.6 4.0 fusion
  910.7 62.4 %all-reduce.15.cloned.1.call-done = f32[512,256]{1,0:T(8,128)} async-done(((f32[512,256]{1,0:T(8,128)}), f32[512,256]{1,0:T(8,128)}) %all-reduce.15.cloned.1.call-update) | async-done | bytes 524304 | tf_op jit(solution)/shard_map/psum | solution.py:28
  974.9 77.1 %all-gather.20.cloned.1.call-done = f32[2048,256]{1,0:T(8,128)} async-done(((f32[64,256]{1,0:T(8,128)}), f32[2048,256]{1,0:T(8,128)}) %all-gather.20.cloned.1.call-update) | async-done | bytes 2097168 | tf_op jit(solution)/shard_map/all_gather | solution.py:92
  1055.2 4.3 all-to-all-start.2
  1059.6 4.1 convolution_bitcast_fusion.1
  1066.9 19.9 %all-to-all-done.2 = f32[4,8,64,256]{3,2,0,1:T(8,128)} async-done(((f32[4,8,64,256]{3,2,0,1:T(8,128)}), f32[4,8,64,256]{3,2,0,1:T(8,128)}, u32[]{:S(2)}, u32[]{:S(2)}) %all-to-all-start.2) | async-done | bytes 2097184 | tf_op jit(solution)/shard_map/all_to_all | solution.py:94
  1088.5 4.0 fusion.2
  1094.1 60.9 %all-reduce.17.cloned.1.call-done = f32[512,256]{1,0:T(8,128)} async-done(((f32[512,256]{1,0:T(8,128)}), f32[512,256]{1,0:T(8,128)}) %all-reduce.17.cloned.1.call-update) | async-done | bytes 524304 | tf_op jit(solution)/shard_map/psum | solution.py:28
  (93 shorter events, 71.9 us)
Async XLA Ops:
  7.2 162.9 %all-reduce.7.cloned.1.call-start = ((), (), s32[]{:S(2)}) async-start(), calls=%async_computation.3 | async-start | bytes 4194304 | tf_op jit(solution)/shard_map/psum | solution.py:22
  14.2 158.1 %copy-start.7 = (f32[4,1,512,256]{3,2,1,0:T(8,128)S(1)}, f32[4,1,512,256]{3,2,1,0:T(8,128)}, u32[]{:S(2)}) copy-start(f32[4,1,512,256]{3,2,1,0:T(8,128)} %param.6) | copy-start | bytes 6291460
  14.2 191.2 %all-gather.10.cloned.1.call-start = ((), (), s32[]{:S(2)}) async-start(), calls=%async_computation.4 | async-start | bytes 4718592 | tf_op jit(solution)/shard_map/all_gather | solution.py:14
  172.3 196.4 %all-reduce.9.cloned.1.call-start = ((), (), s32[]{:S(2)}) async-start(), calls=%async_computation.5 | async-start | bytes 4194304 | tf_op jit(solution)/shard_map/psum | solution.py:22
  215.7 155.4 %copy-start.11 = (f32[1,1,512,256]{3,2,1,0:T(8,128)S(1)}, f32[1,1,512,256]{3,2,1,0:T(8,128)}, u32[]{:S(2)}) copy-start(f32[1,1,512,256]{3,2,1,0:T(8,128)} %get-tuple-element.14) | copy-start | bytes 1572868
  215.7 188.3 %all-gather.12.cloned.1.call-start = ((), (), s32[]{:S(2)}) async-start(), calls=%async_computation.6 | async-start | bytes 4718592 | tf_op jit(solution)/shard_map/all_gather | solution.py:14
  370.8 199.9 %all-reduce.11.cloned.1.call-start = ((), (), s32[]{:S(2)}) async-start(), calls=%async_computation.7 | async-start | bytes 4194304 | tf_op jit(solution)/shard_map/psum | solution.py:22
  417.7 155.2 %copy-start.10 = (f32[1,1,512,256]{3,2,1,0:T(8,128)S(1)}, f32[1,1,512,256]{3,2,1,0:T(8,128)}, u32[]{:S(2)}) copy-start(f32[1,1,512,256]{3,2,1,0:T(8,128)} %get-tuple-element.16) | copy-start | bytes 1572868
  417.7 188.5 %all-gather.14.cloned.1.call-start = ((), (), s32[]{:S(2)}) async-start(), calls=%async_computation.8 | async-start | bytes 4718592 | tf_op jit(solution)/shard_map/all_gather | solution.py:14
  572.8 117.6 %all-gather.16.cloned.1.call-start = ((), (), s32[]{:S(2)}) async-start(), calls=%async_computation.12 | async-start | bytes 2162688 | tf_op jit(solution)/shard_map/all_gather | solution.py:92
  573.0 36.7 %copy-start.4 = (f32[4,1,256,256]{3,2,1,0:T(8,128)S(1)}, f32[4,1,256,256]{3,2,1,0:T(8,128)}, u32[]{:S(2)}) copy-start(f32[4,1,256,256]{3,2,1,0:T(8,128)} %param.7) | copy-start | bytes 3145732
  613.5 176.7 %all-reduce.13.cloned.1.call-start = ((), (), s32[]{:S(2)}) async-start(), calls=%async_computation.9 | async-start | bytes 1048576 | tf_op jit(solution)/shard_map/psum | solution.py:28
  727.8 141.1 %all-gather.18.cloned.1.call-start = ((), (), s32[]{:S(2)}) async-start(), calls=%async_computation.13 | async-start | bytes 2162688 | tf_op jit(solution)/shard_map/all_gather | solution.py:92
  871.9 31.6 %all-to-all-start.1 = ((f32[4,8,64,256]{3,2,0,1:T(8,128)}), f32[4,8,64,256]{3,2,0,1:T(8,128)}, u32[]{:S(2)}, u32[]{:S(2)}) async-start(f32[4,8,64,256]{3,2,0,1:T(8,128)} %copy.21), calls=%async_computation.1 | async-start | bytes 4194304 | tf_op jit(solution)/shard_map/all_to_all | solution.py:94
  876.3 96.7 %all-reduce.15.cloned.1.call-start = ((), (), s32[]{:S(2)}) async-start(), calls=%async_computation.10 | async-start | bytes 1048576 | tf_op jit(solution)/shard_map/psum | solution.py:28
  910.6 141.4 %all-gather.20.cloned.1.call-start = ((), (), s32[]{:S(2)}) async-start(), calls=%async_computation.14 | async-start | bytes 2162688 | tf_op jit(solution)/shard_map/all_gather | solution.py:92
  1055.2 31.6 %all-to-all-start.2 = ((f32[4,8,64,256]{3,2,0,1:T(8,128)}), f32[4,8,64,256]{3,2,0,1:T(8,128)}, u32[]{:S(2)}, u32[]{:S(2)}) async-start(f32[4,8,64,256]{3,2,0,1:T(8,128)} %copy.23), calls=%async_computation.2 | async-start | bytes 4194304 | tf_op jit(solution)/shard_map/all_to_all | solution.py:94
  1059.5 95.5 %all-reduce.17.cloned.1.call-start = ((), (), s32[]{:S(2)}) async-start(), calls=%async_computation.11 | async-start | bytes 1048576 | tf_op jit(solution)/shard_map/psum | solution.py:28
  1059.6 4.1 copy-start.1
  1066.9 21.6 %copy-start.8 = (f32[512,256]{1,0:T(8,128)S(1)}, f32[512,256]{1,0:T(8,128)}, u32[]{:S(2)}) copy-start(f32[512,256]{1,0:T(8,128)} %convolution_bitcast_fusion.1) | copy-start | bytes 1572868
  1088.5 4.1 copy-start.3
  1092.6 63.6 %copy-start.12 = (f32[64,256]{1,0:T(8,128)S(1)}, f32[64,256]{1,0:T(8,128)}, u32[]{:S(2)}) copy-start(f32[64,256]{1,0:T(8,128)} %fusion.33) | copy-start | bytes 196612
  1092.6 63.6 %copy-start.13 = (f32[64,256]{1,0:T(8,128)S(1)}, f32[64,256]{1,0:T(8,128)}, u32[]{:S(2)}) copy-start(f32[64,256]{1,0:T(8,128)} %fusion.36) | copy-start | bytes 196612
  1092.6 63.6 %copy-start.14 = (f32[64,256]{1,0:T(8,128)S(1)}, f32[64,256]{1,0:T(8,128)}, u32[]{:S(2)}) copy-start(f32[64,256]{1,0:T(8,128)} %fusion.39) | copy-start | bytes 196612
  (5 other events, 10.1 us)
Sparse Core Ops, SparseCore 0:
  14.4 155.6 all-reduce.6
  172.4 33.0 all-gather.9
  215.8 152.8 all-reduce.8
  370.9 33.0 all-gather.11
  417.8 152.8 all-reduce.10
  573.1 33.0 all-gather.13
  613.6 76.7 all-gather.15
  727.9 62.2 all-reduce.12
  792.8 75.9 all-gather.17
  910.7 62.2 all-reduce.14
  976.0 75.9 all-gather.19
  1092.7 62.2 all-reduce.16
